TPU v7x, 32 devices: a whole 2x2x4 slice. The times are simulated.
32 devices in a mesh: gy: 1, gx: 32 (over z, y, x, core).
Axes of the slice: x: 2, y: 2, z: 4, core: 2. Of those that a mesh axis runs over, the one named last changes fastest.
Arguments:
- inputs: bfloat16 [32, 2048, 256], P('gy', 'gx'), may hold values from -6 to 6
- cotangent: bfloat16 [32, 2048, 256], P('gy', 'gx'), may hold values from -6 to 6
- mode_weight: bfloat16 [2, 32, 256, 256], P(None, None, 'gx'), may hold values from -2.09375 to 2.09375
- w_in: bfloat16 [256, 1024], replicated, may hold values from -0.375 to 0.375
- w_out: bfloat16 [1024, 256], replicated, may hold values from -0.1875 to 0.1875
Outputs:
- d_inputs: bfloat16 [32, 2048, 256], P('gy', 'gx')
- d_mode: float32 [2, 32, 256, 256], P(None, 'gy', 'gx')
- d_w_in: float32 [256, 1024], P(None, ('gy', 'gx'))
- d_w_out: float32 [1024, 256], P(('gy', 'gx'))
All inputs are finite; a program needn't handle non-finite values.
Results may differ from a plain program's by a relative error of at most 0.014.
Values may be sent and summed in bfloat16 or wider, within the bound.
A program may use at most 64 MiB of HBM per device.

v0:
```python
import math

import jax
import jax.numpy as jnp
from jax import lax
from jax.sharding import PartitionSpec as P

M = 32


def bases(positions, length, modes):
    order = jnp.arange(modes, dtype=jnp.int32)
    phase = positions[:, None] * order[None, :] % length
    angle = phase.astype(jnp.float32) * (2.0 * math.pi / length)
    factor = 1.0 / math.sqrt(length)
    cosine = jnp.cos(angle) * factor
    sine = jnp.sin(angle) * factor
    forward = jnp.concatenate([cosine, -sine], axis=1).astype(jnp.bfloat16)
    weight = jnp.where(order == 0, 1.0, 2.0).astype(jnp.float32)
    inverse = jnp.concatenate([cosine * weight, -sine * weight], axis=1).T.astype(jnp.bfloat16)
    return (forward, inverse)


def smooth_gate(values):
    return jax.nn.gelu(values, approximate=True)


def contract(form, left, right):
    return jnp.einsum(form, left, right, preferred_element_type=jnp.float32)


def local(inputs, cotangent, mode_weight, w_in, w_out):
    line_count, col_count, chan_count = inputs.shape
    x_devices = lax.axis_size("gx")
    y_devices = lax.axis_size("gy")
    own_rows = chan_count // x_devices
    total_x = col_count * x_devices
    positions = lax.axis_index("gx") * col_count + jnp.arange(col_count, dtype=jnp.int32)
    forward, inverse = bases(positions, total_x, M)
    width = 2 * M * line_count
    w_re = mode_weight[0]
    w_im = mode_weight[1]
    piece = inputs
    spectrum = lax.psum_scatter(
        contract("yxc,xm->cmy", piece, forward).reshape(lax.axis_size("gx") * own_rows, width),
        "gx",
        scatter_dimension=0,
        tiled=True,
    ).astype(jnp.bfloat16)
    spectrum = spectrum.reshape(own_rows, 2, M, line_count)
    own_re = spectrum[:, 0]
    own_im = spectrum[:, 1]
    vr = contract("cky,kco->oky", own_re, w_re) - contract("cky,kco->oky", own_im, w_im)
    vi = contract("cky,kco->oky", own_re, w_im) + contract("cky,kco->oky", own_im, w_re)
    mixed = lax.psum(jnp.stack([vr, vi], axis=1).reshape(chan_count, width), "gx").astype(
        jnp.bfloat16
    )
    mixed = mixed.reshape(chan_count, 2 * M, line_count)
    hidden = contract("omy,mx->yxo", mixed, inverse).astype(jnp.bfloat16)
    point_rows = line_count * col_count
    flat_h = hidden.reshape(point_rows, chan_count)
    flat_g = cotangent.reshape(point_rows, chan_count)
    pre = jnp.dot(flat_h, w_in, preferred_element_type=jnp.float32)
    act, pullback = jax.vjp(smooth_gate, pre)
    act = act.astype(jnp.bfloat16)
    grad_out = jnp.dot(act.T, flat_g, preferred_element_type=jnp.float32)
    grad_act = jnp.dot(flat_g, w_out.T, preferred_element_type=jnp.float32)
    d_pre = pullback(grad_act)[0].astype(jnp.bfloat16)
    grad_in = jnp.dot(flat_h.T, d_pre, preferred_element_type=jnp.float32)
    d_hidden = jnp.dot(d_pre, w_in.T, preferred_element_type=jnp.float32).astype(jnp.bfloat16)
    d_hidden = d_hidden.reshape(line_count, col_count, chan_count)
    piece = d_hidden
    d_mixed = lax.psum(
        contract("yxo,mx->omy", piece, inverse).reshape(chan_count, width), "gx"
    ).astype(jnp.bfloat16)
    d_mixed = d_mixed.reshape(chan_count, 2, M, line_count)
    dv_re = d_mixed[:, 0]
    dv_im = d_mixed[:, 1]
    g_re = contract("cky,oky->kco", own_re, dv_re) + contract("cky,oky->kco", own_im, dv_im)
    g_im = contract("cky,oky->kco", own_re, dv_im) - contract("cky,oky->kco", own_im, dv_re)
    mode_grad = jnp.stack([g_re, g_im], axis=0)
    du_re = contract("kco,oky->cky", w_re, dv_re) + contract("kco,oky->cky", w_im, dv_im)
    du_im = contract("kco,oky->cky", w_re, dv_im) - contract("kco,oky->cky", w_im, dv_re)
    coef_local = jnp.stack([du_re, du_im], axis=1).astype(jnp.bfloat16).reshape(own_rows, width)
    coef_all = lax.all_gather(coef_local, "gx", axis=0, tiled=True)
    coef_all = coef_all.reshape(chan_count, 2 * M, line_count)
    returned = contract("cmy,xm->yxc", coef_all, forward)
    d_inputs = (cotangent.astype(jnp.float32) + returned).astype(jnp.bfloat16)
    sum_in, sum_out = (
        lax.psum_scatter(grad_in, ("gy", "gx"), scatter_dimension=1, tiled=True),
        lax.psum_scatter(grad_out, ("gy", "gx"), scatter_dimension=0, tiled=True),
    )
    mode_sum = lax.psum_scatter(
        mode_grad.astype(jnp.bfloat16), "gy", scatter_dimension=1, tiled=True
    ).astype(jnp.float32)
    total_lines = line_count * y_devices
    scale_mlp = 1.0 / math.sqrt(total_lines * total_x)
    scale_mode = 1.0 / math.sqrt(total_lines)
    return (d_inputs, mode_sum * scale_mode, sum_in * scale_mlp, sum_out * scale_mlp)


def solution(mesh):
    placed = (P("gy", "gx", None), P("gy", "gx", None), P(None, None, "gx", None), P(), P())
    return jax.shard_map(
        local,
        mesh=mesh,
        in_specs=placed,
        out_specs=(
            P("gy", "gx", None),
            P(None, "gy", "gx", None),
            P(None, ("gy", "gx")),
            P(("gy", "gx"), None),
        ),
        check_vma=False,
    )
```

profile of v0, /device:TPU:0, one launch (start us, length us, event | category | flops | bytes accessed | tf_op | source)
XLA Modules:
  0.0 621.3 jit_solution(456824582372868959)
XLA Ops:
  7.2 0.0 copy-start
  7.2 0.0 copy-start.4
  7.2 0.0 reduce-scatter.10.cloned.1.call-start
  7.3 0.7 multiply_convert_fusion.3
  8.0 0.4 copy-done
  8.4 0.4 convolution_bitcast_fusion.1
  8.8 1.2 copy.33
  10.0 1.9 copy.48
  11.9 0.0 reduce-scatter.10.cloned.1.call-update
  11.9 0.0 all-gather.2.cloned.1.call-start
  12.0 139.1 %reduce-scatter.10.cloned.1.call-done = f32[8,2048]{1,0:T(8,128)} async-done(((f32[256,2048]{1,0:T(8,128)}), f32[8,2048]{1,0:T(8,128)}) %reduce-scatter.10.cloned.1.call-update) | async-done | bytes 65552 | tf_op jit(solution)/shard_map/reduce_scatter | solution.py:44
  151.1 0.8 convert_element_type.47
  151.9 0.1 reshape.52
  152.1 0.0 copy-done.4
  152.1 0.3 fusion.27
  152.5 0.3 fusion.33
  152.8 0.3 fusion.9
  153.2 0.3 fusion.10
  153.5 0.1 pad_maximum_fusion
  153.7 59.7 %all-reduce.2 = bf16[256,2048]{0,1:T(8,128)(2,1)} all-reduce(f32[256,2048]{0,1:T(8,128)S(1)} %bitcast.113), channel_id=1, replica_groups=mesh['gy'=1,'gx'=32] {'gx'}, use_global_device_ids=true, to_apply=%region_1.2 | all-reduce | flops 524288 | bytes 3145728 | tf_op jit(solution)/shard_map/psum | solution.py:55
  213.4 2.3 convolution_convert_fusion.1
  215.7 2.3 fusion.60
  218.0 0.0 copy-start.1
  218.0 0.0 copy-done.2
  218.0 0.0 copy-done.8
  218.0 0.0 copy-start.5
  218.0 6.4 %fusion.6 = bf16[2048,1024]{1,0:T(8,128)(2,1)S(1)} fusion(f32[2048,1024]{1,0:T(8,128)S(1)} %fusion.60, bf16[2048,256]{1,0:T(8,128)(2,1)S(1)} %bitcast.121, bf16[1024,256]{1,0:T(8,128)(2,1)S(1)} %copy-done.8), kind=kOutput, calls=%fused_computation.8 | convolution fusion | flops 1115684864 | bytes 14155776 | tf_op jit(solution)/shard_map/dot_general | solution.py:67
  224.5 0.0 copy-done.1
  224.5 0.0 copy-done.5
  224.5 0.0 copy-start.9
  224.5 0.0 copy-start.6
  224.5 0.0 copy-start.7
  224.5 1.4 convolution_convert_fusion
  225.9 0.0 copy-done.6
  225.9 0.4 convolution_bitcast_fusion
  226.3 2.5 copy.39
  228.8 0.0 copy-done.9
  228.8 61.3 %all-reduce.3 = bf16[256,2048]{0,1:T(8,128)(2,1)S(1)} all-reduce(f32[256,2048]{0,1:T(8,128)} %bitcast.115), channel_id=1, replica_groups=mesh['gy'=1,'gx'=32] {'gx'}, use_global_device_ids=true, to_apply=%region_2.3 | all-reduce | flops 524288 | bytes 3145728 | tf_op jit(solution)/shard_map/psum | solution.py:73
  290.1 0.2 fusion.24
  290.3 0.2 fusion.22
  290.6 0.3 fusion.17
  290.8 0.3 fusion.18
  291.2 0.8 convert_element_type.54
  292.0 0.0 all-gather.2.cloned.1.call-update
  292.0 0.0 reduce-scatter.6.cloned.1.call-start
  292.0 4.9 fusion.61
  296.9 0.0 reduce-scatter.6.cloned.1.call-update
  297.0 0.0 copy-start.3
  297.0 0.0 reduce-scatter.8.cloned.1.call-start
  297.0 7.6 %fusion.7 = f32[1024,256]{1,0:T(8,128)} fusion(bf16[2048,256]{1,0:T(8,128)(2,1)} %bitcast.120, f32[2048,1024]{1,0:T(8,128)} %copy-done.1), kind=kOutput, calls=%fused_computation.10 | convolution fusion | flops 1092616192 | bytes 10485760 | tf_op jit(solution)/shard_map/dot_general | solution.py:66
  304.6 0.0 reduce-scatter.8.cloned.1.call-update
  304.6 0.2 fusion.23
  304.8 0.2 fusion.13
  305.0 0.2 fusion.21
  305.2 0.2 fusion.14
  305.4 0.8 convert_multiply_fusion
  306.2 38.1 %all-gather.2.cloned.1.call-done = bf16[256,2048]{1,0:T(8,128)(2,1)} async-done(((bf16[8,2048]{1,0:T(8,128)(2,1)}), bf16[256,2048]{1,0:T(8,128)(2,1)}) %all-gather.2.cloned.1.call-update) | async-done | bytes 1048592 | tf_op jit(solution)/shard_map/all_gather | solution.py:85
  344.4 1.5 copy.41
  345.9 0.0 copy-done.3
  345.9 1.9 fusion.8
  347.8 132.7 %reduce-scatter.6.cloned.1.call-done = f32[256,32]{0,1:T(8,128)} async-done(((f32[256,1024]{0,1:T(8,128)}), f32[256,32]{0,1:T(8,128)}) %reduce-scatter.6.cloned.1.call-update) | async-done | bytes 32784 | tf_op jit(solution)/shard_map/reduce_scatter | solution.py:90
  480.5 1.4 broadcast_multiply_fusion.1
  481.9 131.5 %reduce-scatter.8.cloned.1.call-done = f32[32,256]{1,0:T(8,128)} async-done(((f32[1024,256]{1,0:T(8,128)}), f32[32,256]{1,0:T(8,128)}) %reduce-scatter.8.cloned.1.call-update) | async-done | bytes 32784 | tf_op jit(solution)/shard_map/reduce_scatter | solution.py:91
  613.4 1.4 broadcast_multiply_fusion
  (8 shorter events, 0.1 us)
Async XLA Ops:
  7.2 1.2 copy-start
  7.2 144.9 %copy-start.4 = (bf16[2,32,8,256]{3,2,1,0:T(8,128)(2,1)S(1)}, bf16[2,32,8,256]{3,2,1,0:T(8,128)(2,1)}, u32[]{:S(2)}) copy-start(bf16[2,32,8,256]{3,2,1,0:T(8,128)(2,1)} %param.7) | copy-start | bytes 786436
  7.2 143.9 %reduce-scatter.10.cloned.1.call-start = ((), (), s32[]{:S(2)}) async-start(), calls=%async_computation.6 | async-start | bytes 2162688 | tf_op jit(solution)/shard_map/reduce_scatter | solution.py:44
  11.9 332.4 %all-gather.2.cloned.1.call-start = ((), (), s32[]{:S(2)}) async-start(), calls=%async_computation.3 | async-start | bytes 1081344 | tf_op jit(solution)/shard_map/all_gather | solution.py:85
  213.4 4.6 copy-start.2
  213.4 4.6 copy-start.8
  218.0 6.5 %copy-start.1 = (f32[2048,1024]{1,0:T(8,128)}, f32[2048,1024]{1,0:T(8,128)S(1)}, u32[]{:S(2)}) copy-start(f32[2048,1024]{1,0:T(8,128)S(1)} %fusion.60) | copy-start | bytes 25165828
  218.0 6.5 %copy-start.5 = (bf16[256,1024]{1,0:T(8,128)(2,1)S(1)}, bf16[256,1024]{1,0:T(8,128)(2,1)}, u32[]{:S(2)}) copy-start(bf16[256,1024]{1,0:T(8,128)(2,1)} %param.8) | copy-start | bytes 1572868
  224.5 4.4 copy-start.9
  224.5 1.4 copy-start.6
  224.5 1.4 copy-start.7
  292.0 188.5 %reduce-scatter.6.cloned.1.call-start = ((), (), s32[]{:S(2)}) async-start(), calls=%async_computation.4 | async-start | bytes 1081344 | tf_op jit(solution)/shard_map/reduce_scatter | solution.py:90
  297.0 48.9 %copy-start.3 = (bf16[32,64,256]{2,1,0:T(8,128)(2,1)S(1)}, bf16[32,64,256]{2,1,0:T(8,128)(2,1)}, u32[]{:S(2)}) copy-start(bf16[32,64,256]{2,1,0:T(8,128)(2,1)} %param.6) | copy-start | bytes 3145732
  297.0 316.4 %reduce-scatter.8.cloned.1.call-start = ((), (), s32[]{:S(2)}) async-start(), calls=%async_computation.5 | async-start | bytes 1081344 | tf_op jit(solution)/shard_map/reduce_scatter | solution.py:91
Sparse Core Ops, SparseCore 0:
  12.1 138.9 reduce-scatter.9
  292.1 52.2 all-gather.1
  346.7 133.7 reduce-scatter.5
  482.6 130.7 reduce-scatter.7
where the time goes:
time: 622 us; the launch traced here: 621 us
  waiting for transfers between devices  442 us (71%)
  blocking collectives  121 us (19%)
  matrix products  30.7 us (5%)
  between operations  14 us (2%)
  local copies, waits for them, and re-layouts  8.56 us (1%)
    reduce_scatter x1, waiting for transfers between devices, local(): lax.psum_scatter(contract('yxc,xm->cmy', piece, forward).reshape(lax.axis...  139 us
    reduce_scatter x1, waiting for transfers between devices, local(): lax.psum_scatter(grad_in, ('gy', 'gx'), scatter_dimension=1, tiled=True)  133 us
    reduce_scatter x1, waiting for transfers between devices, local(): lax.psum_scatter(grad_out, ('gy', 'gx'), scatter_dimension=0, tiled=True)  131 us
    psum x1, blocking collectives, local(): lax.psum(contract('yxo,mx->omy', piece, inverse).reshape(chan_count, widt...  61.3 us
    psum x1, blocking collectives, local(): lax.psum(jnp.stack([vr, vi], axis=1).reshape(chan_count, width), 'gx')  59.7 us
    all_gather x1, waiting for transfers between devices, local(): coef_all = lax.all_gather(coef_local, 'gx', axis=0, tiled=True)  38.1 us
  transfers between devices with their start and end apart: 4, of which 4 were waited for; matrix products, arithmetic and copies ran while one was open for 3% of the time, Pallas kernels for 0%

commit v1 on v0

--- a/solution.py
+++ b/solution.py
@@ -1,8 +1,11 @@
+import functools
 import math
 
 import jax
 import jax.numpy as jnp
 from jax import lax
+from jax.experimental import pallas as pl
+from jax.experimental.pallas import tpu as pltpu
 from jax.sharding import PartitionSpec as P
 
 M = 32
@@ -29,7 +32,7 @@
     return jnp.einsum(form, left, right, preferred_element_type=jnp.float32)
 
 
-def local(inputs, cotangent, mode_weight, w_in, w_out):
+def local_plain(inputs, cotangent, mode_weight, w_in, w_out):
     line_count, col_count, chan_count = inputs.shape
     x_devices = lax.axis_size("gx")
     y_devices = lax.axis_size("gy")
@@ -99,6 +102,422 @@
     return (d_inputs, mode_sum * scale_mode, sum_in * scale_mlp, sum_out * scale_mlp)
 
 
+CORES = 2
+PLANE = 4
+MESH = pl.DeviceIdType.MESH
+
+
+class Place:
+    def __init__(self, n):
+        me = lax.axis_index("gx")
+        self.depth = n // (CORES * PLANE)
+        self.core = lax.rem(me, CORES)
+        self.chip = lax.rem(lax.div(me, CORES), PLANE)
+        self.z = lax.div(me, CORES * PLANE)
+        self.other = 1 - self.core
+        self.partner = self.at(self.z, self.chip, self.other)
+        self.chips = [lax.rem(self.chip + s, PLANE) for s in range(1, PLANE)]
+        self.order = [lax.rem(self.z + r, self.depth) for r in range(1, self.depth)] + [self.z]
+
+    def at(self, z, chip, core):
+        return (z * PLANE + chip) * CORES + core
+
+    def chip_at(self, chip):
+        return self.at(self.z, chip, self.core)
+
+    def z_at(self, z):
+        return self.at(z, self.chip, self.core)
+
+    def greet(self):
+        peers = [self.partner]
+        peers += [self.chip_at(p) for p in self.chips]
+        peers += [self.z_at(z) for z in self.order[:-1]]
+        barrier = pltpu.get_barrier_semaphore()
+        for peer in peers:
+            pl.semaphore_signal(barrier, inc=1, device_id={"gx": peer}, device_id_type=MESH)
+        pl.semaphore_wait(barrier, len(peers))
+
+
+class Sender:
+    def __init__(self, place, sems):
+        self.place, self.sems, self.used, self.sent = place, sems, 0, []
+
+    def send(self, src, dst, to):
+        copy = pltpu.make_async_remote_copy(
+            src_ref=src,
+            dst_ref=dst,
+            send_sem=self.sems.at[0, self.used],
+            recv_sem=self.sems.at[1, self.used],
+            device_id={"gx": to},
+            device_id_type=MESH,
+        )
+        self.used += 1
+        copy.start()
+        self.sent.append(copy)
+        return copy
+
+    def drain(self):
+        for copy in self.sent:
+            copy.wait_send()
+
+
+class ReduceScatter(Sender):
+    def __init__(self, place, x, bufs):
+        self.x = x
+        self.r1, self.a1, self.r2, self.a2, self.r3, sems = bufs
+        super().__init__(place, sems)
+
+    @staticmethod
+    def scratch(depth, rows, cols):
+        vm = lambda *d: pltpu.VMEM(d + (rows, cols), jnp.bfloat16)
+        count = depth + depth * (PLANE - 1) + depth - 1
+        return [
+            vm(depth, PLANE),
+            vm(depth, PLANE),
+            vm(depth, PLANE - 1),
+            vm(depth),
+            vm(depth),
+            pltpu.SemaphoreType.DMA((2, count)),
+        ]
+
+    def start(self):
+        p = self.place
+        self.c1 = [
+            self.send(self.x.at[zi, :, p.other], self.r1.at[i], p.partner)
+            for i, zi in enumerate(p.order)
+        ]
+
+    def middle(self):
+        p = self.place
+        self.c2 = []
+        for i, zi in enumerate(p.order):
+            self.c1[i].wait_recv()
+            mine = self.x[zi, :, p.core].astype(jnp.float32)
+            self.a1[i] = (mine + self.r1[i].astype(jnp.float32)).astype(jnp.bfloat16)
+            self.c2.append(
+                [
+                    self.send(self.a1.at[i, chip], self.r2.at[i, s], p.chip_at(chip))
+                    for s, chip in enumerate(p.chips)
+                ]
+            )
+
+    def last(self):
+        p = self.place
+        self.c3 = []
+        for i, zi in enumerate(p.order):
+            total = self.a1[i, p.chip].astype(jnp.float32)
+            for s, copy in enumerate(self.c2[i]):
+                copy.wait_recv()
+                total = total + self.r2[i, s].astype(jnp.float32)
+            if i < p.depth - 1:
+                self.a2[i] = total.astype(jnp.bfloat16)
+                self.c3.append(self.send(self.a2.at[i], self.r3.at[i], p.z_at(zi)))
+        self.total = total
+
+    def result(self):
+        total = self.total
+        for i, copy in enumerate(self.c3):
+            copy.wait_recv()
+            total = total + self.r3[i].astype(jnp.float32)
+        return total
+
+
+class AllToAll(Sender):
+    def __init__(self, place, a, out, bufs):
+        self.a, self.out = a, out
+        self.b1, self.b2, sems = bufs
+        super().__init__(place, sems)
+
+    @staticmethod
+    def scratch(depth, rows, cols):
+        vm = lambda *d: pltpu.VMEM(d + (rows, cols), jnp.bfloat16)
+        count = depth + depth * (PLANE - 1) + depth - 1
+        return [
+            vm(depth, CORES, PLANE),
+            vm(depth, PLANE, CORES),
+            pltpu.SemaphoreType.DMA((2, count)),
+        ]
+
+    def start(self):
+        p = self.place
+        self.c1 = [
+            self.send(self.a.at[zi, :, p.other], self.b1.at[i, p.core], p.partner)
+            for i, zi in enumerate(p.order)
+        ]
+        for i, zi in enumerate(p.order):
+            self.b1[i, p.core] = self.a[zi, :, p.core]
+
+    def middle(self):
+        p = self.place
+        self.c2 = []
+        for i in range(p.depth):
+            self.c1[i].wait_recv()
+            self.c2.append(
+                [
+                    self.send(self.b1.at[i, :, chip], self.b2.at[i, p.chip], p.chip_at(chip))
+                    for chip in p.chips
+                ]
+            )
+            self.b2[i, p.chip] = self.b1[i, :, p.chip]
+
+    def last(self):
+        p = self.place
+        self.c3 = []
+        for i, zi in enumerate(p.order):
+            for copy in self.c2[i]:
+                copy.wait_recv()
+            if i < p.depth - 1:
+                self.c3.append(self.send(self.b2.at[i], self.out.at[p.z], p.z_at(zi)))
+            else:
+                self.out[p.z] = self.b2[i]
+
+    def result(self):
+        for copy in self.c3:
+            copy.wait_recv()
+
+
+class AllGather(Sender):
+    def __init__(self, place, out, sems):
+        self.out = out
+        super().__init__(place, sems)
+
+    @staticmethod
+    def scratch(depth):
+        return [pltpu.SemaphoreType.DMA((2, depth * CORES * PLANE - 1))]
+
+    def share(self, z, chip, to):
+        block = self.out.at[z, chip, self.place.core]
+        return self.send(block, block, to)
+
+    def start(self, value):
+        p = self.place
+        self.out[p.z, p.chip, p.core] = value
+        self.c1 = [self.share(p.z, p.chip, p.z_at(zi)) for zi in p.order[:-1]]
+        self.c2, self.c3 = [], []
+        self.forward(p.z)
+
+    def forward(self, z):
+        p = self.place
+        self.c2.append((z, [self.share(z, p.chip, p.chip_at(chip)) for chip in p.chips]))
+        self.c3.append(self.share(z, p.chip, p.partner))
+
+    def middle(self):
+        p = self.place
+        for r, copy in enumerate(self.c1):
+            copy.wait_recv()
+            self.forward(lax.rem(p.z + p.depth - (r + 1), p.depth))
+
+    def last(self):
+        p = self.place
+        for z, copies in self.c2:
+            for s, copy in enumerate(copies):
+                copy.wait_recv()
+                chip = lax.rem(p.chip + PLANE - (s + 1), PLANE)
+                self.c3.append(self.share(z, chip, p.partner))
+
+    def result(self):
+        for copy in self.c3:
+            copy.wait_recv()
+
+
+def mode_matrices(w_ref, chans):
+    depth, plane, cores, rows, width = w_ref.shape
+    both = w_ref[...].astype(jnp.float32).reshape(depth * plane * cores, rows, width)
+    half = rows // 2
+    real = both[:, :half].reshape(chans, width).astype(jnp.bfloat16)
+    imag = both[:, half:].reshape(chans, width).astype(jnp.bfloat16)
+    return real, imag
+
+
+def dot(left, right, dims=((1,), (0,))):
+    return lax.dot_general(left, right, (dims, ((), ())), preferred_element_type=jnp.float32)
+
+
+def forward_kernel(n, x_ref, w_ref, mixed_ref, spec_ref, own_ref, *scratch):
+    place = Place(n)
+    place.greet()
+    sums = ReduceScatter(place, x_ref, scratch[:6])
+    weights = AllToAll(place, w_ref, own_ref, scratch[6:9])
+    gather = AllGather(place, mixed_ref, scratch[9])
+    sums.start()
+    weights.start()
+    sums.middle()
+    weights.middle()
+    sums.last()
+    weights.last()
+    spec = sums.result().astype(jnp.bfloat16)
+    spec_ref[...] = spec
+    weights.result()
+    real, imag = mode_matrices(own_ref, spec.shape[1])
+    by_real, by_imag = dot(spec, real), dot(spec, imag)
+    half = spec.shape[0] // 2
+    vr = by_real[:half] - by_imag[half:]
+    vi = by_imag[:half] + by_real[half:]
+    gather.start(jnp.concatenate([vr, vi], axis=0).astype(jnp.bfloat16))
+    gather.middle()
+    gather.last()
+    gather.result()
+    for part in (sums, weights, gather):
+        part.drain()
+
+
+def backward_kernel(
+    n, x_ref, g_ref, spec_ref, own_ref, coef_ref, mode_ref, grad_ref, give_ref, *scratch
+):
+    place = Place(n)
+    place.greet()
+    sums = ReduceScatter(place, x_ref, scratch[:6])
+    grads = ReduceScatter(place, g_ref, scratch[6:12])
+    modes = AllToAll(place, give_ref, mode_ref, scratch[12:15])
+    gather = AllGather(place, coef_ref, scratch[15])
+    sums.start()
+    grads.start()
+    sums.middle()
+    sums.last()
+    grads.middle()
+    real, imag = mode_matrices(own_ref, spec_ref.shape[1])
+    spec = spec_ref[...]
+    half = spec.shape[0] // 2
+    total = sums.result()
+    dv = total.astype(jnp.bfloat16)
+    by_real = dot(dv, real, ((1,), (1,)))
+    by_imag = dot(dv, imag, ((1,), (1,)))
+    du_re = by_real[:half] + by_imag[half:]
+    du_im = by_real[half:] - by_imag[:half]
+    gather.start(jnp.concatenate([du_re, du_im], axis=0).astype(jnp.bfloat16))
+    turned = jnp.concatenate([total[half:], -total[:half]], axis=0).astype(jnp.bfloat16)
+    g_re = dot(spec, dv, ((0,), (0,)))
+    g_im = dot(spec, turned, ((0,), (0,)))
+    rows = give_ref.shape[3] // 2
+    both = jnp.concatenate(
+        [g_re.reshape(n, rows, -1), g_im.reshape(n, rows, -1)], axis=1
+    ).astype(jnp.bfloat16)
+    give_ref[...] = both.reshape(give_ref.shape)
+    modes.start()
+    gather.middle()
+    grads.last()
+    modes.middle()
+    gather.last()
+    modes.last()
+    grad_ref[...] = grads.result()
+    gather.result()
+    modes.result()
+    for part in (sums, grads, modes, gather):
+        part.drain()
+
+
+def call(kernel, n, outs, scratch, ident, *operands):
+    vmem = pl.BlockSpec(memory_space=pltpu.VMEM)
+    return pl.pallas_call(
+        functools.partial(kernel, n),
+        out_shape=[jax.ShapeDtypeStruct(shape, kind) for shape, kind in outs],
+        in_specs=[vmem] * len(operands),
+        out_specs=[vmem] * len(outs),
+        scratch_shapes=scratch,
+        compiler_params=pltpu.CompilerParams(
+            collective_id=ident, has_side_effects=True, vmem_limit_bytes=40 * 2**20
+        ),
+    )(*operands)
+
+
+def local_by_mode(inputs, cotangent, mode_weight, w_in, w_out):
+    lines, cols, chans = inputs.shape
+    n = lax.axis_size("gx")
+    own = chans // n
+    hid = w_in.shape[1]
+    total_x = cols * n
+    positions = lax.axis_index("gx") * cols + jnp.arange(cols, dtype=jnp.int32)
+    forward, inverse = bases(positions, total_x, M)
+    forward = forward.reshape(cols, 2, M)
+    inverse = inverse.reshape(2, M, cols)
+    depth = n // (CORES * PLANE)
+    grid = (depth, PLANE, CORES)
+    rows = 2 * lines
+    bf = jnp.bfloat16
+    partial_spec = contract("yxc,xrm->mryc", inputs, forward).astype(bf)
+    partial_spec = partial_spec.reshape(grid + (rows, chans))
+    weights = mode_weight.transpose(1, 0, 2, 3).reshape(grid + (2 * own, chans))
+    mixed, spec, own_weights = call(
+        forward_kernel,
+        n,
+        [
+            (grid + (rows, chans), bf),
+            ((rows, chans), bf),
+            (grid + (2 * own, chans), bf),
+        ],
+        ReduceScatter.scratch(depth, rows, chans)
+        + AllToAll.scratch(depth, 2 * own, chans)
+        + AllGather.scratch(depth),
+        0,
+        partial_spec,
+        weights,
+    )
+    mixed = mixed.reshape(M, 2, lines, chans)
+    hidden = contract("mryo,rmx->yxo", mixed, inverse).astype(bf)
+    flat_h = hidden.reshape(lines * cols, chans)
+    flat_g = cotangent.reshape(lines * cols, chans)
+    pre = jnp.dot(flat_h, w_in, preferred_element_type=jnp.float32)
+    act, pullback = jax.vjp(smooth_gate, pre)
+    act = act.astype(bf)
+    grad_out = contract("ph,pc->hc", act, flat_g).astype(bf)
+    grad_act = contract("pc,hc->ph", flat_g, w_out)
+    d_pre = pullback(grad_act)[0].astype(bf)
+    grad_in = contract("ph,pc->hc", d_pre, flat_h).astype(bf)
+    d_hidden = contract("ph,ch->pc", d_pre, w_in).astype(bf)
+    d_hidden = d_hidden.reshape(lines, cols, chans)
+    partial_mixed = contract("yxo,rmx->mryo", d_hidden, inverse).astype(bf)
+    partial_mixed = partial_mixed.reshape(grid + (rows, chans))
+    slab = hid // n
+    grads = jnp.concatenate(
+        [grad_in.reshape(n, slab, chans), grad_out.reshape(n, slab, chans)], axis=1
+    ).reshape(grid + (2 * slab, chans))
+    coef, mode_grad, own_grad = call(
+        backward_kernel,
+        n,
+        [
+            (grid + (rows, chans), bf),
+            (grid + (2 * own, chans), bf),
+            ((2 * slab, chans), jnp.float32),
+        ],
+        [pltpu.VMEM(grid + (2 * own, chans), bf)]
+        + ReduceScatter.scratch(depth, rows, chans)
+        + ReduceScatter.scratch(depth, 2 * slab, chans)
+        + AllToAll.scratch(depth, 2 * own, chans)
+        + AllGather.scratch(depth),
+        1,
+        partial_mixed,
+        grads,
+        spec,
+        own_weights,
+    )
+    returned = contract("mryc,xrm->yxc", coef.reshape(M, 2, lines, chans), forward)
+    d_inputs = (cotangent.astype(jnp.float32) + returned).astype(bf)
+    mode_grad = mode_grad.reshape(M, 2, own, chans).transpose(1, 0, 2, 3).astype(jnp.float32)
+    scale_mlp = 1.0 / math.sqrt(lines * total_x)
+    scale_mode = 1.0 / math.sqrt(lines)
+    return (
+        d_inputs,
+        mode_grad * scale_mode,
+        own_grad[:slab].T * scale_mlp,
+        own_grad[slab:] * scale_mlp,
+    )
+
+
+def local(inputs, cotangent, mode_weight, w_in, w_out):
+    lines, _, chans = inputs.shape
+    n = lax.axis_size("gx")
+    by_mode = (
+        n == M
+        and lax.axis_size("gy") == 1
+        and n % (CORES * PLANE) == 0
+        and chans == 8 * n
+        and w_in.shape[1] % (8 * n) == 0
+        and lines % 8 == 0
+    )
+    plan = local_by_mode if by_mode else local_plain
+    return plan(inputs, cotangent, mode_weight, w_in, w_out)
+
+
 def solution(mesh):
     placed = (P("gy", "gx", None), P("gy", "gx", None), P(None, None, "gx", None), P(), P())
     return jax.shard_map(

time: 622 us -> 91.4 us (0.15)
  waiting for transfers between devices: 442 us -> 0 us
  blocking collectives: 121 us -> 0 us
  Pallas kernels: 0 us -> 68.5 us
  between operations: 14 us -> 0.82 us
  matrix products: 30.7 us -> 17.8 us
    reduce_scatter x3 -> x0, waiting for transfers between devices: 403 us -> none  [the longest x1 139 us: local(): lax.psum_scatter(contract('yxc,xm->cmy', piece, forward).reshape(lax.axis...]
    psum x2 -> x0, blocking collectives: 121 us -> none  [the longest x1 61.3 us: local(): lax.psum(contract('yxo,mx->omy', piece, inverse).reshape(chan_count, widt...]
    pallas_call x0 -> x2, Pallas kernels: none -> 68.5 us  [call(): pl.pallas_call(functools.partial(kernel, n), out_shape=[jax.ShapeDtypeStr...]
    all_gather x1 -> x0, waiting for transfers between devices: 38.1 us -> none  [local(): coef_all = lax.all_gather(coef_local, 'gx', axis=0, tiled=True)]
    dot_general x5 -> x1, matrix products: 22.6 us -> 1.26 us  [local_by_mode(): pre = jnp.dot(flat_h, w_in, preferred_element_type=jnp.float32)]
    dot_general x16 -> x8, matrix products: 8.13 us -> 16.5 us  [contract(): return jnp.einsum(form, left, right, preferred_element_type=jnp.float32)]
  transfers between devices with their start and end apart: 4 -> 0, of which waited for: 4 -> 0; matrix products, arithmetic and copies ran while one was open for 3% -> 0% of each run, Pallas kernels for 0% -> 0%
where the time goes in v1:
time: 91.4 us; the launch traced here: 91.2 us
  Pallas kernels  68.5 us (75%)
  matrix products  17.8 us (19%)
  local copies, waits for them, and re-layouts  3.12 us (3%)
  other arithmetic  0.97 us (1%)
    pallas_call x2, Pallas kernels, call(): pl.pallas_call(functools.partial(kernel, n), out_shape=[jax.ShapeDtypeStr...  68.5 us
    dot_general x8, matrix products, contract(): return jnp.einsum(form, left, right, preferred_element_type=jnp.float32)  16.5 us

profile of v1, /device:TPU:0, one launch (start us, length us, event | category | flops | bytes accessed | tf_op | source)
XLA Modules:
  0.0 91.2 jit_solution(9150886400208792938)
XLA Ops:
  0.6 0.0 copy-start
  0.6 0.0 copy-start.2
  0.7 0.1 multiply_convert_fusion.5
  0.8 0.1 multiply_convert_fusion.6
  0.9 1.1 %copy.10 = bf16[32,2,8,256]{3,2,1,0:T(8,128)(2,1)S(1)} copy(bf16[32,2,8,256]{3,2,0,1:T(8,128)(2,1)} %bitcast.78) | data formatting | bytes 524288 | tf_op jit(solution)/shard_map/transpose | solution.py:439
  2.0 0.0 copy-done
  2.0 0.4 fusion.9
  2.4 0.6 copy.9
  3.0 0.0 copy-start.1
  3.0 34.6 %shard_map.84 = (bf16[4,4,2,64,256]{4,3,2,1,0:T(8,128)(2,1)S(1)}, bf16[64,256]{1,0:T(8,128)(2,1)S(1)}, bf16[4,4,2,16,256]{4,3,2,1,0:T(8,128)(2,1)S(1)}) custom-call(bf16[4,4,2,64,256]{4,3,2,1,0:T(8,128)(2,1)S(1)} %bitcast.65, bf16[4,4,2,16,256]{4,3,2,1,0:T(8,128)(2,1)S(1)} %bitcast.67), custom_call_target="tpu_custom_call" | custom-call | tf_op jit(solution)/shard_map/pallas_call | solution.py:411
  37.6 0.9 bitcast_convert_fusion
  38.5 0.0 copy-done.2
  38.5 1.3 %fusion.35 = f32[2048,1024]{1,0:T(8,128)S(1)} fusion(bf16[2048,256]{1,0:T(8,128)(2,1)S(1)} %bitcast.69, bf16[256,1024]{1,0:T(8,128)(2,1)S(1)} %copy-done.2), kind=kOutput, calls=%fused_computation.64 | convolution fusion | flops 1073741824 | bytes 9961472 | tf_op jit(solution)/shard_map/dot_general | solution.py:459
  39.8 0.0 copy-done.1
  39.8 0.0 copy-start.3
  39.8 3.8 %fusion.11 = bf16[1024,256]{1,0:T(8,128)(2,1)S(1)} fusion(bf16[2048,256]{1,0:T(8,128)(2,1)S(1)} %bitcast.72, f32[2048,1024]{1,0:T(8,128)S(1)} %fusion.35), kind=kOutput, calls=%fused_computation.19 | convolution fusion | flops 1092878336 | bytes 9961472 | tf_op jit(solution)/shard_map/ph,pc->hc/dot_general | solution.py:32
  43.6 0.0 copy-done.3
  43.6 6.4 %fusion.6 = bf16[2048,1024]{1,0:T(8,128)(2,1)S(1)} fusion(f32[2048,1024]{1,0:T(8,128)S(1)} %fusion.35, bf16[2048,256]{1,0:T(8,128)(2,1)S(1)} %bitcast.73, bf16[1024,256]{1,0:T(8,128)(2,1)S(1)} %copy-done.3), kind=kOutput, calls=%fused_computation.8 | convolution fusion | flops 1115684864 | bytes 14155776 | tf_op jit(solution)/shard_map/pc,hc->ph/dot_general | solution.py:32
  50.0 1.3 %convolution_convert_fusion.3 = bf16[1024,256]{1,0:T(8,128)(2,1)S(1)} fusion(bf16[2048,1024]{1,0:T(8,128)(2,1)S(1)} %fusion.6, bf16[2048,256]{1,0:T(8,128)(2,1)S(1)} %bitcast.70), kind=kOutput, calls=%fused_computation.20 | convolution fusion | flops 1074003968 | bytes 5767168 | tf_op jit(solution)/shard_map/ph,pc->hc/dot_general | solution.py:32
  51.4 1.4 %convolution_convert_fusion = bf16[2048,256]{1,0:T(8,128)(2,1)S(1)} fusion(bf16[2048,1024]{1,0:T(8,128)(2,1)S(1)} %fusion.6, bf16[256,1024]{1,0:T(8,128)(2,1)S(1)} %copy-done.2), kind=kOutput, calls=%fused_computation.11 | convolution fusion | flops 1074266112 | bytes 5767168 | tf_op jit(solution)/shard_map/ph,ch->pc/dot_general | solution.py:32
  52.7 0.4 fusion.10
  53.1 0.6 copy.12
  53.7 0.1 pad_maximum_fusion.g_ref
  53.8 33.9 %shard_map.85 = (bf16[4,4,2,64,256]{4,3,2,1,0:T(8,128)(2,1)S(1)}, bf16[4,4,2,16,256]{4,3,2,1,0:T(8,128)(2,1)S(1)}, f32[64,256]{1,0:T(8,128)S(1)}) custom-call(bf16[4,4,2,64,256]{4,3,2,1,0:T(8,128)(2,1)S(1)} %bitcast.64, bf16[4,4,2,64,256]{4,3,2,1,0:T(8,128)(2,1)S(1)} %pad_maximum_fusion.g_ref, bf16[64,256]{1,0:T(8,128)(2,1)S(1)} %get-tuple-element.11.spec_ref, ...), custom_call_target="tpu_custom_call" | custom-call | tf_op jit(solution)/shard_map/pallas_call | solution.py:411
  87.8 1.9 %fusion.8 = bf16[32,64,256]{2,1,0:T(8,128)(2,1)} fusion(bf16[32,64,256]{2,1,0:T(8,128)(2,1)S(1)} %copy-done.1, bf16[32,2,32,256]{3,2,1,0:T(8,128)(2,1)S(1)} %bitcast.66, bf16[64,1,32]{0,2,1:T(8,128)(2,1)S(1)} %get-tuple-element.19, bf16[64,1,32]{0,2,1:T(8,128)(2,1)S(1)} %get-tuple-element.18), kind=kOutput, calls=%fused_computation.13 | convolution fusion | flops 68698112 | bytes 3153920 | tf_op jit(solution)/shard_map/mryc,xrm->yxc/dot_general | solution.py:32
  89.7 0.6 slice_multiply_fusion
  90.3 0.1 convert_multiply_fusion
  90.4 0.8 copy.24
  (3 shorter events, 0.0 us)
Async XLA Ops:
  0.6 1.4 %copy-start = (bf16[32,64,256]{2,1,0:T(8,128)(2,1)S(1)}, bf16[32,64,256]{2,1,0:T(8,128)(2,1)}, u32[]{:S(2)}) copy-start(bf16[32,64,256]{2,1,0:T(8,128)(2,1)} %param.5) | copy-start | bytes 3145732
  0.6 37.9 %copy-start.2 = (bf16[256,1024]{1,0:T(8,128)(2,1)S(1)}, bf16[256,1024]{1,0:T(8,128)(2,1)}, u32[]{:S(2)}) copy-start(bf16[256,1024]{1,0:T(8,128)(2,1)} %param.8) | copy-start | bytes 1572868
  3.0 36.8 %copy-start.1 = (bf16[32,64,256]{2,1,0:T(8,128)(2,1)S(1)}, bf16[32,64,256]{2,1,0:T(8,128)(2,1)}, u32[]{:S(2)}) copy-start(bf16[32,64,256]{2,1,0:T(8,128)(2,1)} %param.6) | copy-start | bytes 3145732
  39.8 3.8 %copy-start.3 = (bf16[1024,256]{1,0:T(8,128)(2,1)S(1)}, bf16[1024,256]{1,0:T(8,128)(2,1)}, u32[]{:S(2)}) copy-start(bf16[1024,256]{1,0:T(8,128)(2,1)} %param.9) | copy-start | bytes 1572868

commit v2 on v1

--- a/solution.py
+++ b/solution.py
@@ -231,45 +231,43 @@
     @staticmethod
     def scratch(depth, rows, cols):
         vm = lambda *d: pltpu.VMEM(d + (rows, cols), jnp.bfloat16)
-        count = depth + depth * (PLANE - 1) + depth - 1
+        count = depth - 1 + depth * (PLANE - 1) + depth
         return [
-            vm(depth, CORES, PLANE),
+            vm(depth, PLANE, CORES),
             vm(depth, PLANE, CORES),
             pltpu.SemaphoreType.DMA((2, count)),
         ]
 
     def start(self):
         p = self.place
-        self.c1 = [
-            self.send(self.a.at[zi, :, p.other], self.b1.at[i, p.core], p.partner)
-            for i, zi in enumerate(p.order)
+        self.c1 = [self.send(self.a.at[zi], self.b1.at[p.z], p.z_at(zi)) for zi in p.order[:-1]]
+        self.c2 = []
+        self.spread(self.a, p.z)
+
+    def spread(self, held, z):
+        p = self.place
+        copies = [
+            self.send(held.at[z, chip], self.b2.at[z, p.chip], p.chip_at(chip)) for chip in p.chips
         ]
-        for i, zi in enumerate(p.order):
-            self.b1[i, p.core] = self.a[zi, :, p.core]
+        self.b2[z, p.chip] = held[z, p.chip]
+        self.c2.append((z, copies))
 
     def middle(self):
         p = self.place
-        self.c2 = []
-        for i in range(p.depth):
-            self.c1[i].wait_recv()
-            self.c2.append(
-                [
-                    self.send(self.b1.at[i, :, chip], self.b2.at[i, p.chip], p.chip_at(chip))
-                    for chip in p.chips
-                ]
+        for r, copy in enumerate(self.c1):
+            copy.wait_recv()
+            self.spread(self.b1, lax.rem(p.z + p.depth - (r + 1), p.depth))
+
+    def last(self):
+        p = self.place
+        self.c3 = []
+        for z, copies in self.c2:
+            for copy in copies:
+                copy.wait_recv()
+            self.c3.append(
+                self.send(self.b2.at[z, :, p.other], self.out.at[z, :, p.core], p.partner)
             )
-            self.b2[i, p.chip] = self.b1[i, :, p.chip]
-
-    def last(self):
-        p = self.place
-        self.c3 = []
-        for i, zi in enumerate(p.order):
-            for copy in self.c2[i]:
-                copy.wait_recv()
-            if i < p.depth - 1:
-                self.c3.append(self.send(self.b2.at[i], self.out.at[p.z], p.z_at(zi)))
-            else:
-                self.out[p.z] = self.b2[i]
+            self.out[z, :, p.core] = self.b2[z, :, p.core]
 
     def result(self):
         for copy in self.c3:
@@ -339,8 +337,8 @@
     sums = ReduceScatter(place, x_ref, scratch[:6])
     weights = AllToAll(place, w_ref, own_ref, scratch[6:9])
     gather = AllGather(place, mixed_ref, scratch[9])
+    weights.start()
     sums.start()
-    weights.start()
     sums.middle()
     weights.middle()
     sums.last()
@@ -406,6 +404,57 @@
         part.drain()
 
 
+def mlp_kernel(h_ref, g_ref, w1_ref, w1t_ref, w2_ref, dh_ref, gin_ref, gout_ref, sum_in, sum_out):
+    points = h_ref.shape[0]
+    hid = w2_ref.shape[0]
+    chunk = math.gcd(points, 512)
+    tile = math.gcd(hid, 256)
+    by_last = ((1,), (1,))
+    root = math.sqrt(2.0 / math.pi)
+    sum_in[...] = jnp.zeros_like(sum_in)
+    sum_out[...] = jnp.zeros_like(sum_out)
+
+    def step(index, carry):
+        rows = pl.ds(pl.multiple_of(index * chunk, chunk), chunk)
+        h, g = h_ref[rows, :], g_ref[rows, :]
+        total = None
+        for start in range(0, hid, tile):
+            part = pl.ds(start, tile)
+            pre = dot(w1t_ref[part, :], h, by_last)
+            grad = dot(w2_ref[part, :], g, by_last)
+            square = pre * pre
+            turn = jnp.tanh(pre * (root + (root * 0.044715) * square))
+            half = 0.5 + 0.5 * turn
+            act = pre * half
+            slope = half + act * (1.0 - turn) * (root + (3.0 * root * 0.044715) * square)
+            d_pre = (grad * slope).astype(jnp.bfloat16)
+            sum_in[part, :] += dot(d_pre, h)
+            sum_out[part, :] += dot(act.astype(jnp.bfloat16), g)
+            back = dot(w1_ref[:, part], d_pre)
+            total = back if total is None else total + back
+        dh_ref[rows, :] = total.T.astype(jnp.bfloat16)
+        return carry
+
+    lax.fori_loop(0, points // chunk, step, 0)
+    gin_ref[...] = sum_in[...].astype(jnp.bfloat16)
+    gout_ref[...] = sum_out[...].astype(jnp.bfloat16)
+
+
+def mlp(flat_h, flat_g, w_in, w_out):
+    vmem = pl.BlockSpec(memory_space=pltpu.VMEM)
+    points, chans = flat_h.shape
+    hid = w_in.shape[1]
+    wide = jax.ShapeDtypeStruct((hid, chans), jnp.bfloat16)
+    return pl.pallas_call(
+        mlp_kernel,
+        out_shape=[jax.ShapeDtypeStruct((points, chans), jnp.bfloat16), wide, wide],
+        in_specs=[vmem] * 5,
+        out_specs=[vmem] * 3,
+        scratch_shapes=[pltpu.VMEM((hid, chans), jnp.float32)] * 2,
+        compiler_params=pltpu.CompilerParams(vmem_limit_bytes=40 * 2**20),
+    )(flat_h, flat_g, w_in, w_in.T, w_out)
+
+
 def call(kernel, n, outs, scratch, ident, *operands):
     vmem = pl.BlockSpec(memory_space=pltpu.VMEM)
     return pl.pallas_call(
@@ -456,14 +505,7 @@
     hidden = contract("mryo,rmx->yxo", mixed, inverse).astype(bf)
     flat_h = hidden.reshape(lines * cols, chans)
     flat_g = cotangent.reshape(lines * cols, chans)
-    pre = jnp.dot(flat_h, w_in, preferred_element_type=jnp.float32)
-    act, pullback = jax.vjp(smooth_gate, pre)
-    act = act.astype(bf)
-    grad_out = contract("ph,pc->hc", act, flat_g).astype(bf)
-    grad_act = contract("pc,hc->ph", flat_g, w_out)
-    d_pre = pullback(grad_act)[0].astype(bf)
-    grad_in = contract("ph,pc->hc", d_pre, flat_h).astype(bf)
-    d_hidden = contract("ph,ch->pc", d_pre, w_in).astype(bf)
+    d_hidden, grad_in, grad_out = mlp(flat_h, flat_g, w_in, w_out)
     d_hidden = d_hidden.reshape(lines, cols, chans)
     partial_mixed = contract("yxo,rmx->mryo", d_hidden, inverse).astype(bf)
     partial_mixed = partial_mixed.reshape(grid + (rows, chans))

time: 91.4 us -> 80.6 us (0.88)
  matrix products: 17.8 us -> 3.64 us
  local copies, waits for them, and re-layouts: 3.12 us -> 4.89 us
  Pallas kernels: 68.5 us -> 70.1 us
    dot_general x8 -> x4, matrix products: 16.5 us -> 3.64 us  [contract(): return jnp.einsum(form, left, right, preferred_element_type=jnp.float32)]
    pallas_call x0 -> x1, Pallas kernels: none -> 10.2 us  [mlp(): pl.pallas_call(mlp_kernel, out_shape=[jax.ShapeDtypeStruct((points, chans...]
    pallas_call x2, Pallas kernels: 68.5 us -> 59.9 us  [call(): pl.pallas_call(functools.partial(kernel, n), out_shape=[jax.ShapeDtypeStr...]
    unnamed x8 -> x9, local copies, waits for them, and re-layouts: 0.03 us -> 1.84 us
    dot_general x1 -> x0, matrix products: 1.26 us -> none  [local_by_mode(): pre = jnp.dot(flat_h, w_in, preferred_element_type=jnp.float32)]
where the time goes in v2:
time: 80.6 us; the launch traced here: 80.4 us
  Pallas kernels  70.1 us (87%)
  local copies, waits for them, and re-layouts  4.89 us (6%)
  matrix products  3.64 us (5%)
  other arithmetic  0.96 us (1%)
    pallas_call x2, Pallas kernels, call(): pl.pallas_call(functools.partial(kernel, n), out_shape=[jax.ShapeDtypeStr...  59.9 us
    pallas_call x1, Pallas kernels, mlp(): pl.pallas_call(mlp_kernel, out_shape=[jax.ShapeDtypeStruct((points, chans...  10.2 us
    dot_general x4, matrix products, contract(): return jnp.einsum(form, left, right, preferred_element_type=jnp.float32)  3.64 us
    unnamed x9, local copies, waits for them, and re-layouts  1.84 us

profile of v2, /device:TPU:0, one launch (start us, length us, event | category | flops | bytes accessed | tf_op | source)
XLA Modules:
  0.0 80.4 jit_solution(12065506871380037848)
XLA Ops:
  0.6 0.0 copy-start
  0.7 0.1 multiply_convert_fusion.1
  0.8 0.1 multiply_convert_fusion.2
  0.9 1.0 %copy.10 = bf16[32,2,8,256]{3,2,1,0:T(8,128)(2,1)S(1)} copy(bf16[32,2,8,256]{3,2,0,1:T(8,128)(2,1)} %bitcast.69) | data formatting | bytes 524288 | tf_op jit(solution)/shard_map/transpose | solution.py:488
  1.9 1.2 %copy.12 = bf16[256,1024]{0,1:T(8,128)(2,1)S(1)} copy(bf16[256,1024]{1,0:T(8,128)(2,1)} %w1_ref.1) | data formatting | bytes 1048576 | tf_op args[3]
  3.2 0.0 copy-done
  3.2 0.4 fusion.1
  3.6 0.6 copy.9
  4.2 29.5 %shard_map.84 = (bf16[4,4,2,64,256]{4,3,2,1,0:T(8,128)(2,1)S(1)}, bf16[64,256]{1,0:T(8,128)(2,1)S(1)}, bf16[4,4,2,16,256]{4,3,2,1,0:T(8,128)(2,1)S(1)}) custom-call(bf16[4,4,2,64,256]{4,3,2,1,0:T(8,128)(2,1)S(1)} %bitcast.59, bf16[4,4,2,16,256]{4,3,2,1,0:T(8,128)(2,1)S(1)} %bitcast.62), custom_call_target="tpu_custom_call" | custom-call | tf_op jit(solution)/shard_map/pallas_call | solution.py:460
  33.7 0.0 copy-start.1
  33.7 0.0 copy-start.2
  33.7 0.0 copy-start.3
  33.7 0.9 %bitcast_convert_fusion = bf16[64,32,256]{2,0,1:T(8,128)(2,1)S(1)} fusion(bf16[2,32,64,1]{2,1,0,3:T(8,128)(2,1)S(1)} %bitcast.70, bf16[32,2,32,256]{3,2,1,0:T(8,128)(2,1)S(1)} %bitcast.64), kind=kOutput, calls=%fused_computation.2 | convolution fusion | flops 67633152 | bytes 2105344 | tf_op jit(solution)/shard_map/mryo,rmx->yxo/dot_general | solution.py:32
  34.6 0.3 copy-done.1
  34.9 0.1 copy-done.2
  35.0 0.2 copy-done.3
  35.2 10.2 %shard_map.85 = (bf16[2048,256]{1,0:T(8,128)(2,1)S(1)}, bf16[1024,256]{1,0:T(8,128)(2,1)S(1)}, bf16[1024,256]{1,0:T(8,128)(2,1)S(1)}) custom-call(bf16[2048,256]{1,0:T(8,128)(2,1)S(1)} %bitcast.57, bf16[2048,256]{1,0:T(8,128)(2,1)S(1)} %bitcast.56, bf16[256,1024]{1,0:T(8,128)(2,1)S(1)} %copy-done.2, bf16[1024,256]{1,0:T(8,128)(2,1)S(1)} %bitcast.60, ...), custom_call_target="tpu_custom_call" | custom-call | tf_op jit(solution)/shard_map/pallas_call | solution.py:448
  45.4 0.4 fusion.2
  45.8 0.6 copy.13
  46.4 0.1 pad_maximum_fusion.g_ref
  46.5 30.4 %shard_map.86 = (bf16[4,4,2,64,256]{4,3,2,1,0:T(8,128)(2,1)S(1)}, bf16[4,4,2,16,256]{4,3,2,1,0:T(8,128)(2,1)S(1)}, f32[64,256]{1,0:T(8,128)S(1)}) custom-call(bf16[4,4,2,64,256]{4,3,2,1,0:T(8,128)(2,1)S(1)} %bitcast.58, bf16[4,4,2,64,256]{4,3,2,1,0:T(8,128)(2,1)S(1)} %pad_maximum_fusion.g_ref, bf16[64,256]{1,0:T(8,128)(2,1)S(1)} %get-tuple-element.17.spec_ref, ...), custom_call_target="tpu_custom_call" | custom-call | tf_op jit(solution)/shard_map/pallas_call | solution.py:460
  77.0 1.9 %fusion = bf16[32,64,256]{2,1,0:T(8,128)(2,1)} fusion(bf16[32,64,256]{2,1,0:T(8,128)(2,1)S(1)} %copy-done.1, bf16[32,2,32,256]{3,2,1,0:T(8,128)(2,1)S(1)} %bitcast.61, bf16[64,1,32]{0,2,1:T(8,128)(2,1)S(1)} %get-tuple-element.25, bf16[64,1,32]{0,2,1:T(8,128)(2,1)S(1)} %get-tuple-element.24), kind=kOutput, calls=%fused_computation.1 | convolution fusion | flops 68698112 | bytes 3153920 | tf_op jit(solution)/shard_map/mryc,xrm->yxc/dot_general | solution.py:32
  78.9 0.6 slice_multiply_fusion
  79.5 0.1 convert_multiply_fusion
  79.6 0.8 %copy.25 = f32[32,2,8,256]{3,2,0,1:T(8,128)} copy(f32[32,2,8,256]{3,2,1,0:T(8,128)S(1)} %bitcast.67) | data formatting | bytes 1048576 | tf_op jit(solution)/shard_map/mul | solution.py:542
  (3 shorter events, 0.0 us)
Async XLA Ops:
  0.6 2.5 %copy-start = (bf16[32,64,256]{2,1,0:T(8,128)(2,1)S(1)}, bf16[32,64,256]{2,1,0:T(8,128)(2,1)}, u32[]{:S(2)}) copy-start(bf16[32,64,256]{2,1,0:T(8,128)(2,1)} %param.5) | copy-start | bytes 3145732
  33.7 1.2 %copy-start.1 = (bf16[32,64,256]{2,1,0:T(8,128)(2,1)S(1)}, bf16[32,64,256]{2,1,0:T(8,128)(2,1)}, u32[]{:S(2)}) copy-start(bf16[32,64,256]{2,1,0:T(8,128)(2,1)} %param.6) | copy-start | bytes 3145732
  33.7 1.3 %copy-start.2 = (bf16[256,1024]{1,0:T(8,128)(2,1)S(1)}, bf16[256,1024]{1,0:T(8,128)(2,1)}, u32[]{:S(2)}) copy-start(bf16[256,1024]{1,0:T(8,128)(2,1)} %w1_ref.1) | copy-start | bytes 1572868
  33.7 1.5 %copy-start.3 = (bf16[1024,256]{1,0:T(8,128)(2,1)S(1)}, bf16[1024,256]{1,0:T(8,128)(2,1)}, u32[]{:S(2)}) copy-start(bf16[1024,256]{1,0:T(8,128)(2,1)} %w2_ref.1) | copy-start | bytes 1572868

commit v3 on v2

--- a/solution.py
+++ b/solution.py
@@ -135,7 +135,10 @@
         barrier = pltpu.get_barrier_semaphore()
         for peer in peers:
             pl.semaphore_signal(barrier, inc=1, device_id={"gx": peer}, device_id_type=MESH)
-        pl.semaphore_wait(barrier, len(peers))
+        self.peers = len(peers)
+
+    def meet(self):
+        pl.semaphore_wait(pltpu.get_barrier_semaphore(), self.peers)
 
 
 class Sender:
@@ -331,14 +334,39 @@
     return lax.dot_general(left, right, (dims, ((), ())), preferred_element_type=jnp.float32)
 
 
-def forward_kernel(n, x_ref, w_ref, mixed_ref, spec_ref, own_ref, *scratch):
+GROUP = 8
+
+
+def group_table(forward):
+    cols, modes = forward.shape
+    lane = jnp.arange(GROUP * cols, dtype=jnp.int32)
+    wide = jnp.tile(forward.T, (1, GROUP))
+    same = jnp.arange(GROUP, dtype=jnp.int32)[:, None] == lane[None, :] // cols
+    table = jnp.where(same[None], wide[:, None, :], jnp.zeros((), forward.dtype))
+    return table.reshape(modes * GROUP, GROUP * cols)
+
+
+def put_modes(stage, group, block):
+    modes, rows, chans = stage.shape
+    parts = block.reshape(2, modes, GROUP, chans)
+    for part in range(2):
+        start = pl.multiple_of(part * (rows // 2) + group * GROUP, GROUP)
+        stage[:, pl.ds(start, GROUP), :] = parts[part]
+
+
+def forward_kernel(n, in_ref, table_ref, w_ref, mixed_ref, spec_ref, own_ref, x_ref, stage, *scratch):
     place = Place(n)
     place.greet()
     sums = ReduceScatter(place, x_ref, scratch[:6])
     weights = AllToAll(place, w_ref, own_ref, scratch[6:9])
     gather = AllGather(place, mixed_ref, scratch[9])
+    chunk = table_ref.shape[1]
+    for group in range(in_ref.shape[0] // chunk):
+        put_modes(stage, group, dot(table_ref[...], in_ref[pl.ds(group * chunk, chunk), :]))
+    x_ref[...] = stage[...].astype(jnp.bfloat16).reshape(x_ref.shape)
+    place.meet()
+    sums.start()
     weights.start()
-    sums.start()
     sums.middle()
     weights.middle()
     sums.last()
@@ -359,8 +387,60 @@
         part.drain()
 
 
+def mlp_steps(h_ref, g_ref, w1_ref, w1t_ref, w2_ref, table_ref, stage, sum_in, sum_out):
+    points = h_ref.shape[0]
+    hid = w2_ref.shape[0]
+    chunk = table_ref.shape[1]
+    tile = math.gcd(hid, 256)
+    by_last = ((1,), (1,))
+    root = math.sqrt(2.0 / math.pi)
+    sum_in[...] = jnp.zeros_like(sum_in)
+    sum_out[...] = jnp.zeros_like(sum_out)
+
+    def step(index, carry):
+        rows = pl.ds(pl.multiple_of(index * chunk, chunk), chunk)
+        h, g = h_ref[rows, :], g_ref[rows, :]
+        total = None
+        for start in range(0, hid, tile):
+            part = pl.ds(start, tile)
+            pre = dot(w1t_ref[part, :], h, by_last)
+            grad = dot(w2_ref[part, :], g, by_last)
+            square = pre * pre
+            turn = jnp.tanh(pre * (root + (root * 0.044715) * square))
+            half = 0.5 + 0.5 * turn
+            act = pre * half
+            slope = half + act * (1.0 - turn) * (root + (3.0 * root * 0.044715) * square)
+            d_pre = (grad * slope).astype(jnp.bfloat16)
+            sum_in[part, :] += dot(d_pre, h)
+            sum_out[part, :] += dot(act.astype(jnp.bfloat16), g)
+            back = dot(w1_ref[:, part], d_pre)
+            total = back if total is None else total + back
+        put_modes(stage, index, dot(table_ref[...], total.astype(jnp.bfloat16), by_last))
+        return carry
+
+    lax.fori_loop(0, points // chunk, step, 0)
+
+
 def backward_kernel(
-    n, x_ref, g_ref, spec_ref, own_ref, coef_ref, mode_ref, grad_ref, give_ref, *scratch
+    n,
+    h_ref,
+    cot_ref,
+    w1_ref,
+    w1t_ref,
+    w2_ref,
+    table_ref,
+    spec_ref,
+    own_ref,
+    coef_ref,
+    mode_ref,
+    grad_ref,
+    x_ref,
+    g_ref,
+    give_ref,
+    stage,
+    sum_in,
+    sum_out,
+    *scratch,
 ):
     place = Place(n)
     place.greet()
@@ -368,7 +448,15 @@
     grads = ReduceScatter(place, g_ref, scratch[6:12])
     modes = AllToAll(place, give_ref, mode_ref, scratch[12:15])
     gather = AllGather(place, coef_ref, scratch[15])
+    mlp_steps(h_ref, cot_ref, w1_ref, w1t_ref, w2_ref, table_ref, stage, sum_in, sum_out)
+    stage[0] = stage[0] * 0.5
+    x_ref[...] = (stage[...] * 2.0).astype(jnp.bfloat16).reshape(x_ref.shape)
+    place.meet()
     sums.start()
+    slab = g_ref.shape[3] // 2
+    shape = g_ref.shape[:3] + (slab, g_ref.shape[4])
+    g_ref[:, :, :, :slab, :] = sum_in[...].astype(jnp.bfloat16).reshape(shape)
+    g_ref[:, :, :, slab:, :] = sum_out[...].astype(jnp.bfloat16).reshape(shape)
     grads.start()
     sums.middle()
     sums.last()
@@ -404,57 +492,6 @@
         part.drain()
 
 
-def mlp_kernel(h_ref, g_ref, w1_ref, w1t_ref, w2_ref, dh_ref, gin_ref, gout_ref, sum_in, sum_out):
-    points = h_ref.shape[0]
-    hid = w2_ref.shape[0]
-    chunk = math.gcd(points, 512)
-    tile = math.gcd(hid, 256)
-    by_last = ((1,), (1,))
-    root = math.sqrt(2.0 / math.pi)
-    sum_in[...] = jnp.zeros_like(sum_in)
-    sum_out[...] = jnp.zeros_like(sum_out)
-
-    def step(index, carry):
-        rows = pl.ds(pl.multiple_of(index * chunk, chunk), chunk)
-        h, g = h_ref[rows, :], g_ref[rows, :]
-        total = None
-        for start in range(0, hid, tile):
-            part = pl.ds(start, tile)
-            pre = dot(w1t_ref[part, :], h, by_last)
-            grad = dot(w2_ref[part, :], g, by_last)
-            square = pre * pre
-            turn = jnp.tanh(pre * (root + (root * 0.044715) * square))
-            half = 0.5 + 0.5 * turn
-            act = pre * half
-            slope = half + act * (1.0 - turn) * (root + (3.0 * root * 0.044715) * square)
-            d_pre = (grad * slope).astype(jnp.bfloat16)
-            sum_in[part, :] += dot(d_pre, h)
-            sum_out[part, :] += dot(act.astype(jnp.bfloat16), g)
-            back = dot(w1_ref[:, part], d_pre)
-            total = back if total is None else total + back
-        dh_ref[rows, :] = total.T.astype(jnp.bfloat16)
-        return carry
-
-    lax.fori_loop(0, points // chunk, step, 0)
-    gin_ref[...] = sum_in[...].astype(jnp.bfloat16)
-    gout_ref[...] = sum_out[...].astype(jnp.bfloat16)
-
-
-def mlp(flat_h, flat_g, w_in, w_out):
-    vmem = pl.BlockSpec(memory_space=pltpu.VMEM)
-    points, chans = flat_h.shape
-    hid = w_in.shape[1]
-    wide = jax.ShapeDtypeStruct((hid, chans), jnp.bfloat16)
-    return pl.pallas_call(
-        mlp_kernel,
-        out_shape=[jax.ShapeDtypeStruct((points, chans), jnp.bfloat16), wide, wide],
-        in_specs=[vmem] * 5,
-        out_specs=[vmem] * 3,
-        scratch_shapes=[pltpu.VMEM((hid, chans), jnp.float32)] * 2,
-        compiler_params=pltpu.CompilerParams(vmem_limit_bytes=40 * 2**20),
-    )(flat_h, flat_g, w_in, w_in.T, w_out)
-
-
 def call(kernel, n, outs, scratch, ident, *operands):
     vmem = pl.BlockSpec(memory_space=pltpu.VMEM)
     return pl.pallas_call(
@@ -464,7 +501,7 @@
         out_specs=[vmem] * len(outs),
         scratch_shapes=scratch,
         compiler_params=pltpu.CompilerParams(
-            collective_id=ident, has_side_effects=True, vmem_limit_bytes=40 * 2**20
+            collective_id=ident, has_side_effects=True, vmem_limit_bytes=(20 + 12 * ident) * 2**20
         ),
     )(*operands)
 
@@ -477,14 +514,13 @@
     total_x = cols * n
     positions = lax.axis_index("gx") * cols + jnp.arange(cols, dtype=jnp.int32)
     forward, inverse = bases(positions, total_x, M)
+    table = group_table(forward)
     forward = forward.reshape(cols, 2, M)
     inverse = inverse.reshape(2, M, cols)
     depth = n // (CORES * PLANE)
     grid = (depth, PLANE, CORES)
     rows = 2 * lines
     bf = jnp.bfloat16
-    partial_spec = contract("yxc,xrm->mryc", inputs, forward).astype(bf)
-    partial_spec = partial_spec.reshape(grid + (rows, chans))
     weights = mode_weight.transpose(1, 0, 2, 3).reshape(grid + (2 * own, chans))
     mixed, spec, own_weights = call(
         forward_kernel,
@@ -494,25 +530,20 @@
             ((rows, chans), bf),
             (grid + (2 * own, chans), bf),
         ],
-        ReduceScatter.scratch(depth, rows, chans)
+        [pltpu.VMEM(grid + (rows, chans), bf), pltpu.VMEM((M, rows, chans), jnp.float32)]
+        + ReduceScatter.scratch(depth, rows, chans)
         + AllToAll.scratch(depth, 2 * own, chans)
         + AllGather.scratch(depth),
         0,
-        partial_spec,
+        inputs.reshape(lines * cols, chans),
+        table,
         weights,
     )
     mixed = mixed.reshape(M, 2, lines, chans)
     hidden = contract("mryo,rmx->yxo", mixed, inverse).astype(bf)
     flat_h = hidden.reshape(lines * cols, chans)
     flat_g = cotangent.reshape(lines * cols, chans)
-    d_hidden, grad_in, grad_out = mlp(flat_h, flat_g, w_in, w_out)
-    d_hidden = d_hidden.reshape(lines, cols, chans)
-    partial_mixed = contract("yxo,rmx->mryo", d_hidden, inverse).astype(bf)
-    partial_mixed = partial_mixed.reshape(grid + (rows, chans))
     slab = hid // n
-    grads = jnp.concatenate(
-        [grad_in.reshape(n, slab, chans), grad_out.reshape(n, slab, chans)], axis=1
-    ).reshape(grid + (2 * slab, chans))
     coef, mode_grad, own_grad = call(
         backward_kernel,
         n,
@@ -521,14 +552,25 @@
             (grid + (2 * own, chans), bf),
             ((2 * slab, chans), jnp.float32),
         ],
-        [pltpu.VMEM(grid + (2 * own, chans), bf)]
+        [
+            pltpu.VMEM(grid + (rows, chans), bf),
+            pltpu.VMEM(grid + (2 * slab, chans), bf),
+            pltpu.VMEM(grid + (2 * own, chans), bf),
+            pltpu.VMEM((M, rows, chans), jnp.float32),
+            pltpu.VMEM((hid, chans), jnp.float32),
+            pltpu.VMEM((hid, chans), jnp.float32),
+        ]
         + ReduceScatter.scratch(depth, rows, chans)
         + ReduceScatter.scratch(depth, 2 * slab, chans)
         + AllToAll.scratch(depth, 2 * own, chans)
         + AllGather.scratch(depth),
         1,
-        partial_mixed,
-        grads,
+        flat_h,
+        flat_g,
+        w_in,
+        w_in.T,
+        w_out,
+        table,
         spec,
         own_weights,
     )
@@ -553,8 +595,10 @@
         and lax.axis_size("gy") == 1
         and n % (CORES * PLANE) == 0
         and chans == 8 * n
-        and w_in.shape[1] % (8 * n) == 0
-        and lines % 8 == 0
+        and w_in.shape[1] % (16 * n) == 0
+        and lines % 16 == 0
+        and inputs.shape[1] % 16 == 0
+        and inputs.shape[1] <= 128
     )
     plan = local_by_mode if by_mode else local_plain
     return plan(inputs, cotangent, mode_weight, w_in, w_out)

time: 80.6 us -> 77.7 us (0.964)
  Pallas kernels: 70.1 us -> 67.6 us
  matrix products: 3.64 us -> 2.83 us
    pallas_call x1 -> x0, Pallas kernels: 10.2 us -> none  [mlp(): pl.pallas_call(mlp_kernel, out_shape=[jax.ShapeDtypeStruct((points, chans...]
    pallas_call x2, Pallas kernels: 59.9 us -> 67.6 us  [call(): pl.pallas_call(functools.partial(kernel, n), out_shape=[jax.ShapeDtypeStr...]
    unnamed x9 -> x13, local copies, waits for them, and re-layouts: 1.84 us -> 4.19 us
    convert_element_type x2 -> x0, local copies, waits for them, and re-layouts: 1.17 us -> none  [the longest x1 0.59 us: local_by_mode(): partial_spec = contract('yxc,xrm->mryc', inputs, forward).astype(bf)]
    transpose x1, local copies, waits for them, and re-layouts: 1.04 us -> 0.02 us  [local_by_mode(): weights = mode_weight.transpose(1, 0, 2, 3).reshape(grid + (2 * own, chans))]
    dot_general x4 -> x2, matrix products: 3.64 us -> 2.83 us  [contract(): return jnp.einsum(form, left, right, preferred_element_type=jnp.float32)]
where the time goes in v3:
time: 77.7 us; the launch traced here: 77.4 us
  Pallas kernels  67.6 us (87%)
  local copies, waits for them, and re-layouts  5.21 us (7%)
  matrix products  2.83 us (4%)
  other arithmetic  0.98 us (1%)
    pallas_call x2, Pallas kernels, call(): pl.pallas_call(functools.partial(kernel, n), out_shape=[jax.ShapeDtypeStr...  67.6 us
    unnamed x13, local copies, waits for them, and re-layouts  4.19 us
    dot_general x2, matrix products, contract(): return jnp.einsum(form, left, right, preferred_element_type=jnp.float32)  2.83 us

profile of v3, /device:TPU:0, one launch (start us, length us, event | category | flops | bytes accessed | tf_op | source)
XLA Modules:
  0.0 77.4 jit_solution(13231074863560558543)
XLA Ops:
  0.6 0.0 copy-start.5
  0.6 0.0 copy-start.3
  0.7 0.1 multiply_convert_fusion
  0.8 0.1 tile.9
  1.0 0.1 select_bitcast_fusion.table_ref
  1.1 0.5 copy-done.5
  1.6 0.3 copy-done.3
  1.9 29.4 %shard_map.84 = (bf16[4,4,2,64,256]{4,3,2,1,0:T(8,128)(2,1)S(1)}, bf16[64,256]{1,0:T(8,128)(2,1)S(1)}, bf16[4,4,2,16,256]{4,3,2,1,0:T(8,128)(2,1)S(1)}) custom-call(bf16[2048,256]{1,0:T(8,128)(2,1)S(1)} %bitcast.43, bf16[512,512]{1,0:T(8,128)(2,1)S(1)} %select_bitcast_fusion.table_ref, bf16[4,4,2,16,256]{4,3,2,1,0:T(8,128)(2,1)S(1)} %bitcast.44), custom_call_target="tpu_custom_call" | custom-call | tf_op jit(solution)/shard_map/pallas_call | solution.py:497
  31.4 0.0 copy-start.1
  31.4 0.9 %bitcast_convert_fusion = bf16[64,32,256]{2,0,1:T(8,128)(2,1)S(1)} fusion(bf16[2,32,64,1]{2,1,0,3:T(8,128)(2,1)S(1)} %bitcast.49, bf16[32,2,32,256]{3,2,1,0:T(8,128)(2,1)S(1)} %bitcast.45), kind=kOutput, calls=%fused_computation.2 | convolution fusion | flops 67633152 | bytes 2105344 | tf_op jit(solution)/shard_map/mryo,rmx->yxo/dot_general | solution.py:32
  32.3 0.0 copy-start
  32.3 0.1 copy-done.1
  32.4 1.0 %copy.11 = bf16[256,1024]{0,1:T(8,128)(2,1)} copy(bf16[256,1024]{1,0:T(8,128)(2,1)S(1)} %copy-done.1) | data formatting | bytes 1048576 | tf_op args[3]
  33.4 0.1 copy-done
  33.6 0.0 copy-start.2
  33.6 1.0 %copy-done.2 = bf16[256,1024]{0,1:T(8,128)(2,1)S(1)} copy-done((bf16[256,1024]{0,1:T(8,128)(2,1)S(1)}, bf16[256,1024]{0,1:T(8,128)(2,1)}, u32[]{:S(2)}) %copy-start.2) | copy-done | bytes 524312
  34.6 0.0 copy-start.4
  34.6 1.0 %copy-done.4 = bf16[1024,256]{1,0:T(8,128)(2,1)S(1)} copy-done((bf16[1024,256]{1,0:T(8,128)(2,1)S(1)}, bf16[1024,256]{1,0:T(8,128)(2,1)}, u32[]{:S(2)}) %copy-start.4) | copy-done | bytes 524312
  35.6 38.2 %shard_map.85 = (bf16[4,4,2,64,256]{4,3,2,1,0:T(8,128)(2,1)S(1)}, bf16[4,4,2,16,256]{4,3,2,1,0:T(8,128)(2,1)S(1)}, f32[64,256]{1,0:T(8,128)S(1)}) custom-call(bf16[2048,256]{1,0:T(8,128)(2,1)S(1)} %bitcast.40, bf16[2048,256]{1,0:T(8,128)(2,1)S(1)} %bitcast.39, bf16[256,1024]{1,0:T(8,128)(2,1)S(1)} %copy-done.1, bf16[1024,256]{1,0:T(8,128)(2,1)S(1)} %bitcast.41, ...), custom_call_target="tpu_custom_call" | custom-call | tf_op jit(solution)/shard_map/pallas_call | solution.py:497
  73.8 0.1 multiply_convert_fusion.3
  73.9 1.9 %fusion = bf16[32,64,256]{2,1,0:T(8,128)(2,1)} fusion(bf16[32,64,256]{2,1,0:T(8,128)(2,1)S(1)} %copy-done, bf16[32,2,32,256]{3,2,1,0:T(8,128)(2,1)S(1)} %bitcast.42, bf16[64,1,32]{0,2,1:T(8,128)(2,1)S(1)} %get-tuple-element.19, bf16[64,1,32]{0,2,1:T(8,128)(2,1)S(1)} %get-tuple-element.18), kind=kOutput, calls=%fused_computation.1 | convolution fusion | flops 68698112 | bytes 3153920 | tf_op jit(solution)/shard_map/mryc,xrm->yxc/dot_general | solution.py:32
  75.9 0.1 convert_multiply_fusion
  75.9 0.8 %copy.21 = f32[32,2,8,256]{3,2,0,1:T(8,128)} copy(f32[32,2,8,256]{3,2,1,0:T(8,128)S(1)} %bitcast.46) | data formatting | bytes 1048576 | tf_op jit(solution)/shard_map/mul | solution.py:584
  76.8 0.6 slice_multiply_fusion
  (8 shorter events, 0.1 us)
Async XLA Ops:
  0.6 1.0 %copy-start.5 = (bf16[2,32,8,256]{3,2,1,0:T(8,128)(2,1)S(1)}, bf16[2,32,8,256]{3,2,1,0:T(8,128)(2,1)}, u32[]{:S(2)}) copy-start(bf16[2,32,8,256]{3,2,1,0:T(8,128)(2,1)} %param.7) | copy-start | bytes 786436
  0.6 1.3 %copy-start.3 = (bf16[32,64,256]{2,1,0:T(8,128)(2,1)S(1)}, bf16[32,64,256]{2,1,0:T(8,128)(2,1)}, u32[]{:S(2)}) copy-start(bf16[32,64,256]{2,1,0:T(8,128)(2,1)} %param.5) | copy-start | bytes 3145732
  31.4 1.0 %copy-start.1 = (bf16[256,1024]{1,0:T(8,128)(2,1)S(1)}, bf16[256,1024]{1,0:T(8,128)(2,1)}, u32[]{:S(2)}) copy-start(bf16[256,1024]{1,0:T(8,128)(2,1)} %w1_ref.1) | copy-start | bytes 1572868
  32.3 1.3 %copy-start = (bf16[32,64,256]{2,1,0:T(8,128)(2,1)S(1)}, bf16[32,64,256]{2,1,0:T(8,128)(2,1)}, u32[]{:S(2)}) copy-start(bf16[32,64,256]{2,1,0:T(8,128)(2,1)} %param.6) | copy-start | bytes 3145732
  33.6 1.0 %copy-start.2 = (bf16[256,1024]{0,1:T(8,128)(2,1)S(1)}, bf16[256,1024]{0,1:T(8,128)(2,1)}, u32[]{:S(2)}) copy-start(bf16[256,1024]{0,1:T(8,128)(2,1)} %copy.11) | copy-start | bytes 1572868
  34.6 1.0 %copy-start.4 = (bf16[1024,256]{1,0:T(8,128)(2,1)S(1)}, bf16[1024,256]{1,0:T(8,128)(2,1)}, u32[]{:S(2)}) copy-start(bf16[1024,256]{1,0:T(8,128)(2,1)} %w2_ref.1) | copy-start | bytes 1572868
